TPU v7x, 512 devices: a whole 4x4x16 slice. The times are simulated.
512 devices in a mesh: dp: 8 (over y, core), expert: 64 (over x, z).
Axes of the slice: x: 4, y: 4, z: 16, core: 2. Of those that a mesh axis runs over, the one named last changes fastest.
Arguments:
- tokens: bfloat16 [64, 64, 3584], P('expert', 'dp'), may hold values from -6 to 6
- grad_out: bfloat16 [64, 64, 3584], P('expert', 'dp'), may hold values from -6 to 6
- routes: int32 [64, 64, 8], P('expert', 'dp'), may hold values from 0 to 255, all different within a row; in each aligned block of 64 rows (0 to 63, 64 to 127, ..., all dimensions but the last counted through in order) at most 4 rows name the same one
- gate_scores: bfloat16 [64, 64, 8], P('expert', 'dp'), may hold values from 0.099609375 to 0.59765625
- w_gate: bfloat16 [64, 3584, 1024], P('expert', None, 'dp'), may hold values from -0.09375 to 0.09375
- w_up: bfloat16 [64, 3584, 1024], P('expert', None, 'dp'), may hold values from -0.09375 to 0.09375
- w_down: bfloat16 [64, 1024, 3584], P('expert', 'dp'), may hold values from -0.1875 to 0.1875
Outputs:
- grad_tokens: bfloat16 [64, 64, 3584], P('expert', 'dp')
- grad_gate: bfloat16 [64, 3584, 1024], P('expert', None, 'dp')
- grad_up: bfloat16 [64, 3584, 1024], P('expert', None, 'dp')
Inputs may be any that keep to these rules, and one draw needn't show every extreme that they name: `routes`: each token names 8 different experts. In each token group of 64 tokens no expert is named by more than 4 tokens, a bound that some block reaches.
All inputs are finite; a program needn't handle non-finite values.
Results may differ from a plain program's by a relative error of at most 0.0058.
Values may be sent and summed in bfloat16 or wider, within the bound.
A program may use at most 64 MiB of HBM per device.

v0:
```python
import jax
import jax.numpy as jnp
from jax import lax
from jax.sharding import PartitionSpec as P

ROUTED = 256


def on_device(tokens, grad_out, routes, gate_scores, w_gate, w_up, w_down):
    groups = lax.axis_size("dp")
    experts = lax.axis_size("expert")
    width = tokens.shape[2]
    top = routes.shape[2]
    tok_col = tokens.shape[1] * groups
    most = max(2, 2 * tok_col * top // ROUTED)
    rows_all = experts * most
    col_x, col_dy, col_scores = (
        lax.all_gather(tokens, "dp", axis=1, tiled=True),
        lax.all_gather(grad_out, "dp", axis=1, tiled=True),
        lax.all_gather(gate_scores, "dp", axis=1, tiled=True),
    )
    col_routes = lax.all_gather(routes, "dp", axis=1, tiled=True)
    col_x = col_x[0]
    col_dy = col_dy[0]
    flat_routes = col_routes[0].reshape(-1)
    flat_scores = col_scores[0].reshape(-1).astype(jnp.float32)
    onehot = (flat_routes[:, None] == jnp.arange(experts, dtype=jnp.int32)[None, :]).astype(
        jnp.int32
    )
    place = jnp.sum(onehot * (jnp.cumsum(onehot, axis=0) - 1), axis=1)
    inside = flat_routes < experts
    target = jnp.where(inside, flat_routes * most + place, -1).reshape(tok_col, top)
    match = jnp.arange(rows_all, dtype=jnp.int32)[:, None, None] == target[None, :, :]
    select = jnp.sum(match.astype(jnp.float32), axis=2)
    weight = jnp.sum(
        match.astype(jnp.float32) * flat_scores.reshape(tok_col, top)[None, :, :], axis=(1, 2)
    )
    select_half = select.astype(jnp.bfloat16)
    send_x = jnp.dot(select_half, col_x, preferred_element_type=jnp.float32).astype(jnp.bfloat16)
    send_g = (
        weight[:, None] * jnp.dot(select_half, col_dy, preferred_element_type=jnp.float32)
    ).astype(jnp.bfloat16)
    send_x = send_x.reshape(experts, most, width)
    send_g = send_g.reshape(experts, most, width)
    recv_x, recv_g = (
        lax.all_to_all(send_x, "expert", split_axis=0, concat_axis=0, tiled=True),
        lax.all_to_all(send_g, "expert", split_axis=0, concat_axis=0, tiled=True),
    )
    rows = recv_x.reshape(rows_all, width)
    scaled = recv_g.reshape(rows_all, width)
    wgate = w_gate[0]
    wup = w_up[0]
    wdown = w_down[0]
    gate = jnp.dot(rows, wgate, preferred_element_type=jnp.float32)
    up = jnp.dot(rows, wup, preferred_element_type=jnp.float32)
    dhidden = jnp.einsum("rd,fd->rf", scaled, wdown, preferred_element_type=jnp.float32)
    sig = jax.nn.sigmoid(gate)
    dgate = (dhidden * up * sig * (1.0 + gate * (1.0 - sig))).astype(jnp.bfloat16)
    dup = (dhidden * gate * sig).astype(jnp.bfloat16)
    partial_value = jnp.einsum("rf,df->rd", dgate, wgate, preferred_element_type=jnp.float32)
    partial_value = partial_value + jnp.einsum(
        "rf,df->rd", dup, wup, preferred_element_type=jnp.float32
    )
    grad_g = jnp.einsum("rd,rf->df", rows, dgate, preferred_element_type=jnp.float32).astype(
        jnp.bfloat16
    )
    grad_u = jnp.einsum("rd,rf->df", rows, dup, preferred_element_type=jnp.float32).astype(
        jnp.bfloat16
    )
    back = lax.all_to_all(
        partial_value.reshape(experts, most, width),
        "expert",
        split_axis=0,
        concat_axis=0,
        tiled=True,
    )
    gathered = jnp.dot(select.T, back.reshape(rows_all, width), precision=lax.Precision.HIGHEST)
    mine = lax.psum_scatter(gathered, "dp", scatter_dimension=0, tiled=True)
    grad_tokens = mine.astype(jnp.bfloat16)[None]
    return (grad_tokens, grad_g[None], grad_u[None])


def solution(mesh):
    placed = (
        P("expert", "dp", None),
        P("expert", "dp", None),
        P("expert", "dp", None),
        P("expert", "dp", None),
        P("expert", None, "dp"),
        P("expert", None, "dp"),
        P("expert", "dp", None),
    )
    return jax.shard_map(
        on_device,
        mesh=mesh,
        in_specs=placed,
        out_specs=(P("expert", "dp", None), P("expert", None, "dp"), P("expert", None, "dp")),
        check_vma=False,
    )
```

profile of v0, /device:TPU:1, one launch (start us, length us, event | category | flops | bytes accessed | tf_op | source)
XLA Modules:
  0.0 490.1 jit_solution(12948847612415215358)
XLA Ops:
  7.2 19.8 %all_gather.12 = s32[1,64,8]{2,1,0:T(8,128)S(1)} all-gather(s32[1,8,8]{2,1,0:T(8,128)} %param.9), channel_id=1, replica_groups=mesh['dp'=8,'expert'=64] {'dp'}, dimensions={1}, use_global_device_ids=true | all-gather | bytes 2304 | tf_op jit(solution)/shard_map/all_gather | solution.py:22
  27.1 11.4 %all_gather.13 = bf16[1,64,8]{2,1,0:T(8,128)(2,1)S(1)} all-gather(bf16[1,8,8]{2,1,0:T(8,128)(2,1)} %param.10), channel_id=1, replica_groups=mesh['dp'=8,'expert'=64] {'dp'}, dimensions={1}, use_global_device_ids=true | all-gather | bytes 1152 | tf_op jit(solution)/shard_map/all_gather | solution.py:20
  40.2 13.3 %all_gather.15 = bf16[1,64,3584]{2,1,0:T(8,128)(2,1)S(1)} all-gather(bf16[1,8,3584]{2,1,0:T(8,128)(2,1)} %param.7), channel_id=1, replica_groups=mesh['dp'=8,'expert'=64] {'dp'}, dimensions={1}, use_global_device_ids=true | all-gather | bytes 516096 | tf_op jit(solution)/shard_map/all_gather | solution.py:18
  54.5 1.5 reshape.48
  55.9 13.6 %all-to-all-start.1 = ((bf16[64,4,3584]{2,1,0:T(4,128)(2,1)}), bf16[64,4,3584]{2,1,0:T(4,128)(2,1)S(1)}, u32[]{:S(2)}, u32[]{:S(2)}) async-start(bf16[64,4,3584]{2,1,0:T(4,128)(2,1)} %reshape.48), calls=%async_computation.1 | async-start | bytes 3670016 | tf_op jit(solution)/shard_map/all_to_all | solution.py:46
  69.5 13.3 %all_gather.14 = bf16[1,64,3584]{2,1,0:T(8,128)(2,1)S(1)} all-gather(bf16[1,8,3584]{2,1,0:T(8,128)(2,1)S(1)} %copy-done.3), channel_id=1, replica_groups=mesh['dp'=8,'expert'=64] {'dp'}, dimensions={1}, use_global_device_ids=true | all-gather | bytes 516096 | tf_op jit(solution)/shard_map/all_gather | solution.py:19
  82.8 1.9 fusion
  84.7 4.1 reshape.46
  88.9 62.4 %all-to-all-done.1 = bf16[64,4,3584]{2,1,0:T(4,128)(2,1)S(1)} async-done(((bf16[64,4,3584]{2,1,0:T(4,128)(2,1)}), bf16[64,4,3584]{2,1,0:T(4,128)(2,1)S(1)}, u32[]{:S(2)}, u32[]{:S(2)}) %all-to-all-start.1) | async-done | bytes 1835040 | tf_op jit(solution)/shard_map/all_to_all | solution.py:46
  151.2 1.3 copy-done.1
  152.5 12.9 %all-to-all-start = ((bf16[64,4,3584]{2,1,0:T(4,128)(2,1)}), bf16[64,4,3584]{2,1,0:T(4,128)(2,1)}, u32[]{:S(2)}, u32[]{:S(2)}) async-start(bf16[64,4,3584]{2,1,0:T(4,128)(2,1)} %reshape.46), calls=%async_computation | async-start | bytes 3670016 | tf_op jit(solution)/shard_map/all_to_all | solution.py:47
  165.5 2.9 reshape.49
  169.1 77.8 %all-to-all-done = bf16[64,4,3584]{2,1,0:T(4,128)(2,1)} async-done(((bf16[64,4,3584]{2,1,0:T(4,128)(2,1)}), bf16[64,4,3584]{2,1,0:T(4,128)(2,1)}, u32[]{:S(2)}, u32[]{:S(2)}) %all-to-all-start) | async-done | bytes 1835040 | tf_op jit(solution)/shard_map/all_to_all | solution.py:47
  246.9 4.0 reshape.47
  250.9 2.4 multiply_convert_fusion
  254.6 2.5 convolution_add_fusion
  257.1 5.2 %reshape.50 = f32[64,4,3584]{2,1,0:T(4,128)} reshape(f32[256,3584]{1,0:T(8,128)} %convolution_add_fusion) | data formatting | bytes 7340032 | tf_op jit(solution)/shard_map/reshape | solution.py:71
  262.3 173.5 %all_to_all.15 = f32[64,4,3584]{2,1,0:T(4,128)} all-to-all(f32[64,4,3584]{2,1,0:T(4,128)} %reshape.50), channel_id=1, replica_groups=mesh['dp'=8,'expert'=64] {'expert'}, dimensions={0} | all-to-all | bytes 7340032 | tf_op jit(solution)/shard_map/all_to_all | solution.py:70
  435.8 5.3 %reshape.51 = f32[256,3584]{1,0:T(8,128)} reshape(f32[64,4,3584]{2,1,0:T(4,128)} %all_to_all.15) | data formatting | bytes 7340032 | tf_op jit(solution)/shard_map/reshape | solution.py:77
  441.1 5.3 %fusion.21 = f32[64,3584]{1,0:T(8,128)} fusion(f32[256,64]{0,1:T(8,128)S(1)} %get-tuple-element.4, f32[256,3584]{1,0:T(8,128)} %reshape.51), kind=kOutput, calls=%fused_computation.40 | convolution fusion | flops 704643072 | bytes 4653056 | tf_op jit(solution)/shard_map/dot_general | solution.py:77
  446.4 1.6 fusion.1
  448.0 1.6 fusion.2
  449.6 32.1 %reduce-scatter.2.cloned.1.call-done = f32[8,3584]{1,0:T(8,128)} async-done(((f32[64,3584]{1,0:T(8,128)}), f32[8,3584]{1,0:T(8,128)}) %reduce-scatter.2.cloned.1.call-update) | async-done | bytes 114704 | tf_op jit(solution)/shard_map/reduce_scatter | solution.py:78
  481.7 1.5 convert_bitcast_fusion
  (25 shorter events, 4.8 us)
Async XLA Ops:
  7.2 161.3 %copy-start = (bf16[1,3584,128]{2,1,0:T(8,128)(2,1)S(1)}, bf16[1,3584,128]{2,1,0:T(8,128)(2,1)}, u32[]{:S(2)}) copy-start(bf16[1,3584,128]{2,1,0:T(8,128)(2,1)} %param.11) | copy-start | bytes 2752516
  55.9 13.6 %copy-start.3 = (bf16[1,8,3584]{2,1,0:T(8,128)(2,1)S(1)}, bf16[1,8,3584]{2,1,0:T(8,128)(2,1)}, u32[]{:S(2)}) copy-start(bf16[1,8,3584]{2,1,0:T(8,128)(2,1)} %param.8) | copy-start | bytes 172036
  55.9 95.3 %all-to-all-start.1 = ((bf16[64,4,3584]{2,1,0:T(4,128)(2,1)}), bf16[64,4,3584]{2,1,0:T(4,128)(2,1)S(1)}, u32[]{:S(2)}, u32[]{:S(2)}) async-start(bf16[64,4,3584]{2,1,0:T(4,128)(2,1)} %reshape.48), calls=%async_computation.1 | async-start | bytes 3670016 | tf_op jit(solution)/shard_map/all_to_all | solution.py:46
  151.2 1.3 copy-start.1
  152.5 94.4 %all-to-all-start = ((bf16[64,4,3584]{2,1,0:T(4,128)(2,1)}), bf16[64,4,3584]{2,1,0:T(4,128)(2,1)}, u32[]{:S(2)}, u32[]{:S(2)}) async-start(bf16[64,4,3584]{2,1,0:T(4,128)(2,1)} %reshape.46), calls=%async_computation | async-start | bytes 3670016 | tf_op jit(solution)/shard_map/all_to_all | solution.py:47
  165.4 316.3 %reduce-scatter.2.cloned.1.call-start = ((), (), s32[]{:S(2)}) async-start(), calls=%async_computation.4 | async-start | bytes 1032192 | tf_op jit(solution)/shard_map/reduce_scatter | solution.py:78
  250.9 2.4 copy-start.2
Sparse Core Ops, SparseCore 0:
  446.5 35.2 reduce-scatter.1
where the time goes:
time: 492 us; the launch traced here: 490 us
  blocking collectives  231 us (47%)
  waiting for transfers between devices  172 us (35%)
  starting transfers between devices  26.5 us (5%)
  local copies, waits for them, and re-layouts  24.7 us (5%)
  matrix products  17.9 us (4%)
  between operations  14.1 us (3%)
    all_to_all x1, blocking collectives, on_device(): lax.all_to_all(partial_value.reshape(experts, most, width), 'expert', spl...  174 us
    all_to_all x1, waiting for transfers between devices, on_device(): lax.all_to_all(send_g, 'expert', split_axis=0, concat_axis=0, tiled=True)  77.8 us
    all_to_all x1, waiting for transfers between devices, on_device(): lax.all_to_all(send_x, 'expert', split_axis=0, concat_axis=0, tiled=True)  62.4 us
    reduce_scatter x1, waiting for transfers between devices, on_device(): mine = lax.psum_scatter(gathered, 'dp', scatter_dimension=0, tiled=True)  32.1 us
    all_gather x1, blocking collectives, on_device(): col_routes = lax.all_gather(routes, 'dp', axis=1, tiled=True)  19.8 us
    all_to_all x1, starting transfers between devices, on_device(): lax.all_to_all(send_x, 'expert', split_axis=0, concat_axis=0, tiled=True)  13.6 us
    all_gather x1, blocking collectives, on_device(): lax.all_gather(grad_out, 'dp', axis=1, tiled=True)  13.3 us
    all_gather x1, blocking collectives, on_device(): lax.all_gather(tokens, 'dp', axis=1, tiled=True)  13.3 us
  transfers between devices with their start and end apart: 3, of which 3 were waited for; matrix products, arithmetic and copies ran while one was open for 3% of the time, Pallas kernels for 0%

commit v1 on v0

v1 whole, which is shorter than its diff:
```python
import functools

import jax
import jax.numpy as jnp
from jax import lax
from jax.experimental import pallas as pl
from jax.experimental.pallas import tpu as pltpu
from jax.sharding import PartitionSpec as P

ROUTED = 256
CORES = 2
QUARTERS = 4
MESH = pl.DeviceIdType.MESH
F32, BF16 = jnp.float32, jnp.bfloat16
NT = (((1,), (1,)), ((), ()))
TN = (((0,), (0,)), ((), ()))


def shape_of(mesh_experts, columns_z, width, tok_col, top, hidden):
    z_size = columns_z
    x_size = mesh_experts // z_size
    most = max(2, 2 * tok_col * top // ROUTED)
    quarter = width // QUARTERS
    tiles = quarter // 128
    wide = (tiles + 1) // 2 * 128
    parts = min(4, z_size)
    return dict(
        xs=x_size, zs=z_size, most=most, qw=quarter, wide=wide, parts=parts,
        slots=mesh_experts // parts, experts=mesh_experts, toks=tok_col, top=top, hid=hidden,
    )


def kernel(
    c, tok_ref, dy_ref, routes_ref, scores_ref, wg_hbm, wu_hbm, wd_hbm,
    out_t, out_g, out_u,
    wcat, wd, sa, ra, si, ri, sb, rb, dd, keep, sr1, rr1, sr2, rr2, sr3, rr3, sf, rf, sel_ref,
    w_sem, sa_sem, ra_sem, si_sem, ri_sem, sb_sem, rb_sem,
    sy_sem, ry_sem, sc_sem, rc_sem, s1_sem, r1_sem, s2_sem, r2_sem, s3_sem, r3_sem,
    sf_sem, rf_sem,
):
    xs, zs, most, qw, wide, parts = c["xs"], c["zs"], c["most"], c["qw"], c["wide"], c["parts"]
    slots, experts, toks, hid = c["slots"], c["experts"], c["toks"], c["hid"]
    narrow = qw - wide
    rows = slots * most
    groups = CORES * QUARTERS
    per = toks // groups
    d = lax.axis_index("dp")
    e = lax.axis_index("expert")
    y, core = d // CORES, d % CORES
    x, z = e // zs, e % zs
    other = y * CORES + (1 - core)
    up_y, down_y = (y + 1) % QUARTERS, (y + QUARTERS - 1) % QUARTERS
    far_y = (y + 2) % QUARTERS
    up, down = up_y * CORES + core, down_y * CORES + core

    def remote(src, dst, send, recv, **where):
        return pltpu.make_async_remote_copy(
            src_ref=src, dst_ref=dst, send_sem=send, recv_sem=recv,
            device_id=where, device_id_type=MESH,
        )

    def landed(ref, sem):
        pltpu.make_async_copy(ref, ref, sem).wait()

    loads = [
        pltpu.make_async_copy(wg_hbm.at[0], wcat.at[:, 0:hid], w_sem.at[0]),
        pltpu.make_async_copy(wu_hbm.at[0], wcat.at[:, hid : 2 * hid], w_sem.at[1]),
        pltpu.make_async_copy(wd_hbm.at[0], wd, w_sem.at[2]),
    ]
    for load in loads:
        load.start()

    barrier = pltpu.get_barrier_semaphore()
    for j in range(1, groups):
        pl.semaphore_signal(
            barrier, inc=1, device_id={"dp": (d + j) % groups}, device_id_type=MESH
        )

    def greet(j, carry):
        pl.semaphore_signal(
            barrier, inc=1, device_id={"expert": (e + j) % experts}, device_id_type=MESH
        )
        return carry

    lax.fori_loop(1, experts, greet, 0)

    si[...] = jnp.zeros(si.shape, F32)
    si[0, :, 0 : c["top"]] = routes_ref[0].astype(F32)
    si[1, :, 0 : c["top"]] = scores_ref[0].astype(F32)
    for p in range(groups):
        source = tok_ref if p % CORES == 0 else dy_ref
        at = p // CORES * qw
        sa[p] = source[0, :, at : at + qw]
    ri[d] = si[...]
    ra[d] = sa[d]
    pl.semaphore_wait(barrier, groups - 1 + experts - 1)

    sent_i, sent_a = [], []
    for j in range(1, groups):
        p = (d + j) % groups
        sent_i.append(remote(si, ri.at[d], si_sem.at[j - 1], ri_sem.at[j - 1], dp=p))
        sent_i[-1].start()
    for j in range(1, groups):
        p = (d + j) % groups
        sent_a.append(remote(sa.at[p], ra.at[d], sa_sem.at[j - 1], ra_sem.at[j - 1], dp=p))
        sent_a[-1].start()
    for j in range(1, groups):
        landed(ri.at[(d + groups - j) % groups], ri_sem.at[j - 1])

    route = ri[:, 0].reshape(toks, 128)
    score = ri[:, 1].reshape(toks, 128)
    shape = (toks, experts * most)
    row = lax.broadcasted_iota(jnp.int32, shape, 1)
    place_of = row % most
    slot_of = row // most
    dx_of = slot_of % xs
    k_of = slot_of // xs
    dz_of = (k_of + 1) // 2 * (2 * (k_of % 2) - 1)
    target = ((x + dx_of) % xs * zs + (z + dz_of + zs) % zs).astype(F32)
    hit = jnp.zeros(shape, F32)
    weight = jnp.zeros(shape, F32)
    for k in range(c["top"]):
        same = route[:, k : k + 1] == target
        hit = jnp.where(same, 1.0, hit)
        weight = jnp.where(same, score[:, k : k + 1], weight)
    before = (
        lax.broadcasted_iota(jnp.int32, (toks, toks), 1)
        < lax.broadcasted_iota(jnp.int32, (toks, toks), 0)
    ).astype(F32).astype(BF16)
    place = jnp.dot(before, hit.astype(BF16), preferred_element_type=F32)
    chosen = jnp.where(place == place_of.astype(F32), hit, 0.0)
    sel_ref[...] = chosen.astype(BF16)
    is_x = core == 0
    scaled = jnp.where(is_x, chosen, chosen * weight).astype(BF16)

    for j in range(1, groups):
        landed(ra.at[(d + groups - j) % groups], ra_sem.at[j - 1])
    picked = lax.dot_general(
        scaled, ra[...].reshape(toks, qw), TN, preferred_element_type=F32
    ).astype(BF16)
    sb[...] = picked.reshape(experts, most, qw)
    rb[core, y, 0] = picked[0:most]

    def target_of(i, sign):
        k, dx = i // xs, i % xs
        dz = (k + 1) // 2 * (2 * (k % 2) - 1) * sign
        return (x + sign * dx + xs) % xs * zs + (z + dz + zs) % zs

    for g in range(parts):
        def send_rows(i, carry, g=g):
            remote(
                sb.at[i], rb.at[core, y, i], sb_sem.at[g], rb_sem.at[g],
                expert=target_of(i, 1),
            ).start()
            return carry

        lax.fori_loop(max(1, g * slots), (g + 1) * slots, send_rows, 0)

    first = [max(1, g * slots) for g in range(parts)]

    def part(g, low=0, high=None):
        low, high = g * slots + low, g * slots + (slots if high is None else high)
        return pl.ds(low, high - low)

    half = slots // 2
    pending = []

    def go(copy):
        copy.start()
        pending.append(copy)

    def stage_own(g):
        count = (g + 1) * slots - first[g]
        landed(rb.at[core, y, pl.ds(first[g], count)], rb_sem.at[g])
        mine = rb.at[core, y, part(g)]
        go(remote(mine, mine, sy_sem.at[g, 0], ry_sem.at[g, 0], dp=up))
        go(remote(mine, mine, sy_sem.at[g, 1], ry_sem.at[g, 1], dp=down))
        go(remote(mine, mine, sc_sem.at[g, 0], rc_sem.at[g, 0], dp=other))

    def stage_near(g):
        low = rb.at[core, down_y, part(g)]
        landed(low, ry_sem.at[g, 0])
        piece = rb.at[core, down_y, part(g, 0, half)]
        go(remote(piece, piece, sy_sem.at[g, 2], ry_sem.at[g, 2], dp=up))
        go(remote(low, low, sc_sem.at[g, 1], rc_sem.at[g, 1], dp=other))
        high = rb.at[core, up_y, part(g)]
        landed(high, ry_sem.at[g, 1])
        piece = rb.at[core, up_y, part(g, half)]
        go(remote(piece, piece, sy_sem.at[g, 3], ry_sem.at[g, 3], dp=down))
        go(remote(high, high, sc_sem.at[g, 2], rc_sem.at[g, 2], dp=other))

    def stage_far(g):
        landed(rb.at[core, far_y, part(g, 0, half)], ry_sem.at[g, 2])
        landed(rb.at[core, far_y, part(g, half)], ry_sem.at[g, 3])
        whole = rb.at[core, far_y, part(g)]
        go(remote(whole, whole, sc_sem.at[g, 3], rc_sem.at[g, 3], dp=other))

    def stage_compute(g):
        if g == 0:
            for load in loads:
                load.wait()
        for at, which in enumerate((y, down_y, up_y, far_y)):
            landed(rb.at[1 - core, which, part(g)], rc_sem.at[g, at])
        gu = jnp.zeros((rows, 2 * hid), F32)
        dh = jnp.zeros((rows, hid), F32)
        for q in range(QUARTERS):
            cols = slice(q * qw, (q + 1) * qw)
            gu += jnp.dot(
                rb[0, q, part(g)].reshape(rows, qw), wcat[cols, :], preferred_element_type=F32
            )
            dh += lax.dot_general(
                rb[1, q, part(g)].reshape(rows, qw), wd[:, cols], NT, preferred_element_type=F32
            )
        gate, upv = gu[:, 0:hid], gu[:, hid : 2 * hid]
        sig = jax.nn.sigmoid(gate)
        dgate = dh * upv * sig * (1.0 + gate * (1.0 - sig))
        dup = dh * gate * sig
        both = jnp.concatenate([dgate.astype(BF16), dup.astype(BF16)], axis=1)
        dd[g * rows : (g + 1) * rows, :] = both
        for q in range(QUARTERS):
            back = lax.dot_general(
                both, wcat[q * qw : (q + 1) * qw, :], NT, preferred_element_type=F32
            )
            left = back[:, 0:wide]
            right = back[:, wide:qw]
            if narrow < wide:
                right = jnp.concatenate([right, jnp.zeros((rows, wide - narrow), F32)], axis=1)
            keep[g, q] = jnp.where(is_x, left, right)
            sr1[g, q] = jnp.where(is_x, right, left).astype(BF16)
        go(remote(sr1.at[g], rr1.at[g], s1_sem.at[g], r1_sem.at[g], dp=other))

    def stage_chip(g):
        landed(rr1.at[g], r1_sem.at[g])
        for q in range(QUARTERS):
            sr2[g, q] = (keep[g, q] + rr1[g, q].astype(F32)).astype(BF16)
        for j in range(1, QUARTERS):
            to = (y + j) % QUARTERS
            go(remote(
                sr2.at[g, to], rr2.at[g, j - 1], s2_sem.at[g, j - 1], r2_sem.at[g, j - 1],
                dp=to * CORES + core,
            ))

    def stage_back(g):
        for j in range(1, QUARTERS):
            landed(rr2.at[g, j - 1], r2_sem.at[g, j - 1])
        total = keep[g, y] + rr1[g, y].astype(F32)
        for j in range(1, QUARTERS):
            total += rr2[g, j - 1].astype(F32)
        total = total.astype(BF16)
        sr3[part(g)] = total.reshape(slots, most, wide)
        if g == 0:
            rr3[0] = total[0:most]

        def send_back(i, carry):
            remote(
                sr3.at[i], rr3.at[i], s3_sem.at[g], r3_sem.at[g], expert=target_of(i, -1)
            ).start()
            return carry

        lax.fori_loop(first[g], (g + 1) * slots, send_back, 0)

    def weight_grads(q):
        grads = lax.dot_general(
            rb[0, q].reshape(experts * most, qw), dd[...], TN, preferred_element_type=F32
        )
        out_g[0, q * qw : (q + 1) * qw, :] = grads[:, 0:hid].astype(BF16)
        out_u[0, q * qw : (q + 1) * qw, :] = grads[:, hid : 2 * hid].astype(BF16)

    stages = (stage_own, stage_near, stage_far, stage_compute, stage_chip, stage_back)
    for step in range(parts + len(stages) - 1):
        for lag, stage in enumerate(stages):
            if 0 <= step - lag < parts:
                stage(step - lag)
        done = step - (parts - 1) - 3
        if done == 0:
            weight_grads(0)
        elif done == 1:
            weight_grads(1)
        elif done == 2:
            weight_grads(2)
            weight_grads(3)

    summed = jnp.zeros((toks, wide), F32)
    for g in range(parts):
        count = (g + 1) * slots - first[g]
        landed(rr3.at[pl.ds(first[g], count)], r3_sem.at[g])
        summed += jnp.dot(
            sel_ref[:, g * rows : (g + 1) * rows],
            rr3[part(g)].reshape(rows, wide),
            preferred_element_type=F32,
        )
    sf[...] = summed.astype(BF16).reshape(groups, per, wide)
    rf[d] = sf[d]
    for j in range(1, groups):
        p = (d + j) % groups
        go(remote(sf.at[p], rf.at[d], sf_sem.at[j - 1], rf_sem.at[j - 1], dp=p))
    for copy in sent_i + sent_a + pending[: -(groups - 1)]:
        copy.wait_send()
    for g in range(parts):
        count = (g + 1) * slots - first[g]
        landed(sb.at[pl.ds(first[g], count)], sb_sem.at[g])
        landed(sr3.at[pl.ds(first[g], count)], s3_sem.at[g])
    for j in range(1, groups):
        landed(rf.at[(d + groups - j) % groups], rf_sem.at[j - 1])
    for p in range(groups):
        at, size = p // CORES * qw + p % CORES * wide, (wide, narrow)[p % CORES]
        out_t[0, :, at : at + size] = rf[p, :, 0:size]
    for copy in pending[-(groups - 1) :]:
        copy.wait_send()


def on_device(z_size, tokens, grad_out, routes, gate_scores, w_gate, w_up, w_down):
    groups = lax.axis_size("dp")
    experts = lax.axis_size("expert")
    per, width = tokens.shape[1:]
    hid = w_gate.shape[2]
    toks = per * groups
    c = shape_of(experts, z_size, width, toks, routes.shape[2], hid)
    most, qw, wide, parts, slots = c["most"], c["qw"], c["wide"], c["parts"], c["slots"]
    rows = slots * most
    vmem = pl.BlockSpec(memory_space=pltpu.VMEM)
    hbm = pl.BlockSpec(memory_space=pl.ANY)
    dma = pltpu.SemaphoreType.DMA
    return pl.pallas_call(
        functools.partial(kernel, c),
        out_shape=(
            jax.ShapeDtypeStruct(tokens.shape, BF16),
            jax.ShapeDtypeStruct(w_gate.shape, BF16),
            jax.ShapeDtypeStruct(w_up.shape, BF16),
        ),
        in_specs=[vmem] * 4 + [hbm] * 3,
        out_specs=(vmem, vmem, vmem),
        scratch_shapes=[
            pltpu.VMEM((width, 2 * hid), BF16),
            pltpu.VMEM((hid, width), BF16),
            pltpu.VMEM((groups, per, qw), BF16),
            pltpu.VMEM((groups, per, qw), BF16),
            pltpu.VMEM((2, per, 128), F32),
            pltpu.VMEM((groups, 2, per, 128), F32),
            pltpu.VMEM((experts, most, qw), BF16),
            pltpu.VMEM((CORES, QUARTERS, experts, most, qw), BF16),
            pltpu.VMEM((experts * most, 2 * hid), BF16),
            pltpu.VMEM((parts, QUARTERS, rows, wide), F32),
            pltpu.VMEM((parts, QUARTERS, rows, wide), BF16),
            pltpu.VMEM((parts, QUARTERS, rows, wide), BF16),
            pltpu.VMEM((parts, QUARTERS, rows, wide), BF16),
            pltpu.VMEM((parts, QUARTERS - 1, rows, wide), BF16),
            pltpu.VMEM((experts, most, wide), BF16),
            pltpu.VMEM((experts, most, wide), BF16),
            pltpu.VMEM((groups, per, wide), BF16),
            pltpu.VMEM((groups, per, wide), BF16),
            pltpu.VMEM((toks, experts * most), BF16),
            dma((3,)),
            dma((groups - 1,)),
            dma((groups - 1,)),
            dma((groups - 1,)),
            dma((groups - 1,)),
            dma((parts,)),
            dma((parts,)),
            dma((parts, 4)),
            dma((parts, 4)),
            dma((parts, 4)),
            dma((parts, 4)),
            dma((parts,)),
            dma((parts,)),
            dma((parts, 3)),
            dma((parts, 3)),
            dma((parts,)),
            dma((parts,)),
            dma((groups - 1,)),
            dma((groups - 1,)),
        ],
        compiler_params=pltpu.CompilerParams(
            collective_id=0, has_side_effects=True, vmem_limit_bytes=48 * 1024 * 1024
        ),
        cost_estimate=pl.CostEstimate(
            flops=14 * experts * most * width * hid, bytes_accessed=10 * width * hid,
            transcendentals=experts * most * hid,
        ),
    )(tokens, grad_out, routes, gate_scores, w_gate, w_up, w_down)


def solution(mesh):
    placed = (
        P("expert", "dp", None),
        P("expert", "dp", None),
        P("expert", "dp", None),
        P("expert", "dp", None),
        P("expert", None, "dp"),
        P("expert", None, "dp"),
        P("expert", "dp", None),
    )
    z_size = 16 if mesh.shape["expert"] == 64 else 2
    return jax.shard_map(
        functools.partial(on_device, z_size),
        mesh=mesh,
        in_specs=placed,
        out_specs=(P("expert", "dp", None), P("expert", None, "dp"), P("expert", None, "dp")),
        check_vma=False,
    )
```

time: 492 us -> 98 us (0.20)
  blocking collectives: 231 us -> 0 us
  waiting for transfers between devices: 172 us -> 0 us
  Pallas kernels: 0 us -> 87 us
  starting transfers between devices: 26.5 us -> 0 us
  matrix products: 17.9 us -> 0 us
  local copies, waits for them, and re-layouts: 24.7 us -> 9 us
  between operations: 14.1 us -> 0.66 us
    all_to_all x1 -> x0, blocking collectives: 174 us -> none  [on_device(): lax.all_to_all(partial_value.reshape(experts, most, width), 'expert', spl...]
    all_to_all x2 -> x0, waiting for transfers between devices: 140 us -> none  [the longest x1 77.8 us: on_device(): lax.all_to_all(send_g, 'expert', split_axis=0, concat_axis=0, tiled=True)]
    pallas_call x0 -> x1, Pallas kernels: none -> 87 us  [on_device(): pl.pallas_call(functools.partial(kernel, c), out_shape=(jax.ShapeDtypeStr...]
    all_gather x4 -> x0, blocking collectives: 57.8 us -> none  [the longest x1 19.8 us: on_device(): col_routes = lax.all_gather(routes, 'dp', axis=1, tiled=True)]
    reduce_scatter x1 -> x0, waiting for transfers between devices: 32.1 us -> none  [on_device(): mine = lax.psum_scatter(gathered, 'dp', scatter_dimension=0, tiled=True)]
    all_to_all x2 -> x0, starting transfers between devices: 26.5 us -> none  [the longest x1 13.6 us: on_device(): lax.all_to_all(send_x, 'expert', split_axis=0, concat_axis=0, tiled=True)]
    reshape x6 -> x0, local copies, waits for them, and re-layouts: 22.9 us -> none  [the longest x1 5.26 us: on_device(): back.reshape(rows_all, width)]
    dot_general x10 -> x0, matrix products: 17.9 us -> none  [the longest x1 5.26 us: on_device(): jnp.dot(select.T, back.reshape(rows_all, width), precision=lax.Precision....]
  transfers between devices with their start and end apart: 3 -> 0, of which waited for: 3 -> 0; matrix products, arithmetic and copies ran while one was open for 3% -> 0% of each run, Pallas kernels for 0% -> 0%
where the time goes in v1:
time: 98 us; the launch traced here: 96.7 us
  Pallas kernels  87 us (89%)
  local copies, waits for them, and re-layouts  9 us (9%)
    pallas_call x1, Pallas kernels, on_device(): pl.pallas_call(functools.partial(kernel, c), out_shape=(jax.ShapeDtypeStr...  87 us
    unnamed x17, local copies, waits for them, and re-layouts  9 us

profile of v1, /device:TPU:1, one launch (start us, length us, event | category | flops | bytes accessed | tf_op | source)
XLA Modules:
  0.0 96.7 jit_solution(8771146383626410323)
XLA Ops:
  0.6 0.0 copy-start
  0.6 1.2 %copy-done = bf16[1,3584,128]{2,1,0:T(8,128)(2,1)S(1)} copy-done((bf16[1,3584,128]{2,1,0:T(8,128)(2,1)S(1)}, bf16[1,3584,128]{2,1,0:T(8,128)(2,1)}, u32[]{:S(2)}) %copy-start) | copy-done | bytes 917528
  1.8 0.0 copy-start.1
  1.8 1.2 %copy-done.1 = bf16[1,3584,128]{2,1,0:T(8,128)(2,1)S(1)} copy-done((bf16[1,3584,128]{2,1,0:T(8,128)(2,1)S(1)}, bf16[1,3584,128]{2,1,0:T(8,128)(2,1)}, u32[]{:S(2)}) %copy-start.1) | copy-done | bytes 917528
  3.0 0.0 copy-start.2
  3.0 1.2 %copy-done.2 = bf16[1,128,3584]{2,1,0:T(8,128)(2,1)S(1)} copy-done((bf16[1,128,3584]{2,1,0:T(8,128)(2,1)S(1)}, bf16[1,128,3584]{2,1,0:T(8,128)(2,1)}, u32[]{:S(2)}) %copy-start.2) | copy-done | bytes 917528
  4.2 0.0 copy-start.3
  4.2 0.8 copy-done.3
  5.0 0.0 copy-start.4
  5.0 0.8 copy-done.4
  5.8 0.0 copy-start.5
  5.8 0.7 copy-done.5
  6.5 0.0 copy-start.6
  6.5 0.7 copy-done.6
  7.2 87.0 %shard_map.94 = (bf16[1,8,3584]{2,1,0:T(8,128)(2,1)S(1)}, bf16[1,3584,128]{2,1,0:T(8,128)(2,1)S(1)}, bf16[1,3584,128]{2,1,0:T(8,128)(2,1)S(1)}) custom-call(bf16[1,8,3584]{2,1,0:T(8,128)(2,1)S(1)} %copy-done.3, bf16[1,8,3584]{2,1,0:T(8,128)(2,1)S(1)} %copy-done.4, s32[1,8,8]{2,1,0:T(8,128)S(1)} %copy-done.5, bf16[1,8,8]{2,1,0:T(8,128)(2,1)S(1)} %copy-done.6, ...), custom_call_target="tpu_custom_call" | custom-call | flops 1644167168 | bytes 4587520 | tf_op jit(solution)/shard_map/pallas_call | solution.py:324
  94.2 0.6 copy.13
  94.8 0.9 copy.14
  95.7 0.9 copy.15
Async XLA Ops:
  0.6 1.2 %copy-start = (bf16[1,3584,128]{2,1,0:T(8,128)(2,1)S(1)}, bf16[1,3584,128]{2,1,0:T(8,128)(2,1)}, u32[]{:S(2)}) copy-start(bf16[1,3584,128]{2,1,0:T(8,128)(2,1)} %wg_hbm.1) | copy-start | bytes 2752516
  1.8 1.2 %copy-start.1 = (bf16[1,3584,128]{2,1,0:T(8,128)(2,1)S(1)}, bf16[1,3584,128]{2,1,0:T(8,128)(2,1)}, u32[]{:S(2)}) copy-start(bf16[1,3584,128]{2,1,0:T(8,128)(2,1)} %wu_hbm.1) | copy-start | bytes 2752516
  3.0 1.2 %copy-start.2 = (bf16[1,128,3584]{2,1,0:T(8,128)(2,1)S(1)}, bf16[1,128,3584]{2,1,0:T(8,128)(2,1)}, u32[]{:S(2)}) copy-start(bf16[1,128,3584]{2,1,0:T(8,128)(2,1)} %wd_hbm.1) | copy-start | bytes 2752516
  4.2 0.8 copy-start.3
  5.0 0.8 copy-start.4
  5.8 0.7 copy-start.5
  6.5 0.7 copy-start.6

commit v2 on v1

--- a/solution.py
+++ b/solution.py
@@ -10,10 +10,19 @@
 ROUTED = 256
 CORES = 2
 QUARTERS = 4
+PARTS = 8
 MESH = pl.DeviceIdType.MESH
 F32, BF16 = jnp.float32, jnp.bfloat16
 NT = (((1,), (1,)), ((), ()))
 TN = (((0,), (0,)), ((), ()))
+
+
+def order_of(z_size):
+    steps = [0]
+    for h in range(1, z_size // 2 + 1):
+        steps += [h] if 2 * h == z_size else [h, -h]
+    far = sorted(steps, key=lambda s: (-abs(s), -s))
+    return far[::-1]
 
 
 def shape_of(mesh_experts, columns_z, width, tok_col, top, hidden):
@@ -23,34 +32,38 @@
     quarter = width // QUARTERS
     tiles = quarter // 128
     wide = (tiles + 1) // 2 * 128
-    parts = min(4, z_size)
+    parts = min(PARTS, z_size)
     return dict(
-        xs=x_size, zs=z_size, most=most, qw=quarter, wide=wide, parts=parts,
+        order=order_of(z_size), xs=x_size, zs=z_size, most=most, qw=quarter, wide=wide, parts=parts,
         slots=mesh_experts // parts, experts=mesh_experts, toks=tok_col, top=top, hid=hidden,
     )
 
 
 def kernel(
-    c, tok_ref, dy_ref, routes_ref, scores_ref, wg_hbm, wu_hbm, wd_hbm,
+    c, tok_hbm, dy_hbm, routes_hbm, scores_hbm, wg_hbm, wu_hbm, wd_hbm,
     out_t, out_g, out_u,
-    wcat, wd, sa, ra, si, ri, sb, rb, dd, keep, sr1, rr1, sr2, rr2, sr3, rr3, sf, rf, sel_ref,
-    w_sem, sa_sem, ra_sem, si_sem, ri_sem, sb_sem, rb_sem,
+    wcat, wd, sa, ra, sb, rb, dd, keep, sr1, rr1, sr2, rr2, sr3, rr3, sf, rf, sel_ref,
+    tok_ref, dy_ref, routes_ref, scores_ref, in_sem, w_sem, ring_sem, sa_sem, ra_sem, sb_sem, rb_sem,
     sy_sem, ry_sem, sc_sem, rc_sem, s1_sem, r1_sem, s2_sem, r2_sem, s3_sem, r3_sem,
     sf_sem, rf_sem,
 ):
     xs, zs, most, qw, wide, parts = c["xs"], c["zs"], c["most"], c["qw"], c["wide"], c["parts"]
     slots, experts, toks, hid = c["slots"], c["experts"], c["toks"], c["hid"]
     narrow = qw - wide
+    order = c["order"]
+    own_slot = order.index(0) * xs
+    top = c["top"]
     rows = slots * most
     groups = CORES * QUARTERS
     per = toks // groups
     d = lax.axis_index("dp")
     e = lax.axis_index("expert")
-    y, core = d // CORES, d % CORES
-    x, z = e // zs, e % zs
+    rem, div = lax.rem, lax.div
+    y, core = div(d, CORES), rem(d, CORES)
+    x, z = div(e, zs), rem(e, zs)
     other = y * CORES + (1 - core)
-    up_y, down_y = (y + 1) % QUARTERS, (y + QUARTERS - 1) % QUARTERS
-    far_y = (y + 2) % QUARTERS
+    up_y, down_y = rem(y + 1, QUARTERS), rem(y + QUARTERS - 1, QUARTERS)
+    far_y = rem(y + 2, QUARTERS)
     up, down = up_y * CORES + core, down_y * CORES + core
 
     def remote(src, dst, send, recv, **where):
@@ -62,6 +75,15 @@
     def landed(ref, sem):
         pltpu.make_async_copy(ref, ref, sem).wait()
 
+    small = [
+        pltpu.make_async_copy(src, dst, in_sem.at[i])
+        for i, (src, dst) in enumerate((
+            (routes_hbm, routes_ref), (scores_hbm, scores_ref),
+            (tok_hbm, tok_ref), (dy_hbm, dy_ref),
+        ))
+    ]
+    for load in small:
+        load.start()
     loads = [
         pltpu.make_async_copy(wg_hbm.at[0], wcat.at[:, 0:hid], w_sem.at[0]),
         pltpu.make_async_copy(wu_hbm.at[0], wcat.at[:, hid : 2 * hid], w_sem.at[1]),
@@ -73,90 +95,104 @@
     barrier = pltpu.get_barrier_semaphore()
     for j in range(1, groups):
         pl.semaphore_signal(
-            barrier, inc=1, device_id={"dp": (d + j) % groups}, device_id_type=MESH
+            barrier, inc=1, device_id={"dp": rem(d + j, groups)}, device_id_type=MESH
+        )
+
+    for j in range(1, xs):
+        pl.semaphore_signal(
+            barrier, inc=1, device_id={"expert": rem(x + j, xs) * zs + z}, device_id_type=MESH
         )
 
     def greet(j, carry):
         pl.semaphore_signal(
-            barrier, inc=1, device_id={"expert": (e + j) % experts}, device_id_type=MESH
+            barrier, inc=1, device_id={"expert": x * zs + rem(z + j, zs)}, device_id_type=MESH
         )
         return carry
 
-    lax.fori_loop(1, experts, greet, 0)
-
-    si[...] = jnp.zeros(si.shape, F32)
-    si[0, :, 0 : c["top"]] = routes_ref[0].astype(F32)
-    si[1, :, 0 : c["top"]] = scores_ref[0].astype(F32)
+    lax.fori_loop(1, zs, greet, 0)
+
+    for load in small:
+        load.wait()
     for p in range(groups):
         source = tok_ref if p % CORES == 0 else dy_ref
         at = p // CORES * qw
-        sa[p] = source[0, :, at : at + qw]
-    ri[d] = si[...]
+        sa[p, :, 0:qw] = source[0, :, at : at + qw]
+        sa[p, :, qw : qw + top] = routes_ref[0].astype(F32).astype(BF16)
+        sa[p, :, qw + 128 : qw + 128 + top] = scores_ref[0]
     ra[d] = sa[d]
-    pl.semaphore_wait(barrier, groups - 1 + experts - 1)
-
-    sent_i, sent_a = [], []
+    pl.semaphore_wait(barrier, groups - 1 + xs - 1 + zs - 1)
+
+    sent_a = []
     for j in range(1, groups):
-        p = (d + j) % groups
-        sent_i.append(remote(si, ri.at[d], si_sem.at[j - 1], ri_sem.at[j - 1], dp=p))
-        sent_i[-1].start()
-    for j in range(1, groups):
-        p = (d + j) % groups
+        p = rem(d + j, groups)
         sent_a.append(remote(sa.at[p], ra.at[d], sa_sem.at[j - 1], ra_sem.at[j - 1], dp=p))
         sent_a[-1].start()
-    for j in range(1, groups):
-        landed(ri.at[(d + groups - j) % groups], ri_sem.at[j - 1])
-
-    route = ri[:, 0].reshape(toks, 128)
-    score = ri[:, 1].reshape(toks, 128)
+    for j in range(1, xs):
+        pl.semaphore_signal(
+            ring_sem, inc=1, device_id={"expert": rem(x + j, xs) * zs + z}, device_id_type=MESH
+        )
+
     shape = (toks, experts * most)
     row = lax.broadcasted_iota(jnp.int32, shape, 1)
-    place_of = row % most
-    slot_of = row // most
-    dx_of = slot_of % xs
-    k_of = slot_of // xs
-    dz_of = (k_of + 1) // 2 * (2 * (k_of % 2) - 1)
-    target = ((x + dx_of) % xs * zs + (z + dz_of + zs) % zs).astype(F32)
+    place_of = row & (most - 1)
+    slot_of = row >> (most.bit_length() - 1)
+    dx_of = slot_of & (xs - 1)
+    k_of = slot_of >> (xs.bit_length() - 1)
+    dz_of = jnp.zeros(shape, jnp.int32)
+    for k, dz in enumerate(order):
+        dz_of = jnp.where(k_of == k, dz, dz_of)
+    target = (((x + dx_of) & (xs - 1)) * zs + ((z + dz_of) & (zs - 1))).astype(F32)
+    before = (
+        lax.broadcasted_iota(jnp.int32, (toks, toks), 1)
+        < lax.broadcasted_iota(jnp.int32, (toks, toks), 0)
+    ).astype(F32).astype(BF16)
+    for j in range(1, groups):
+        landed(ra.at[rem(d + groups - j, groups)], ra_sem.at[j - 1])
+    route = ra[:, :, qw : qw + 128].reshape(toks, 128).astype(F32)
+    score = ra[:, :, qw + 128 : qw + 256].reshape(toks, 128).astype(F32)
     hit = jnp.zeros(shape, F32)
     weight = jnp.zeros(shape, F32)
     for k in range(c["top"]):
         same = route[:, k : k + 1] == target
         hit = jnp.where(same, 1.0, hit)
         weight = jnp.where(same, score[:, k : k + 1], weight)
-    before = (
-        lax.broadcasted_iota(jnp.int32, (toks, toks), 1)
-        < lax.broadcasted_iota(jnp.int32, (toks, toks), 0)
-    ).astype(F32).astype(BF16)
     place = jnp.dot(before, hit.astype(BF16), preferred_element_type=F32)
     chosen = jnp.where(place == place_of.astype(F32), hit, 0.0)
     sel_ref[...] = chosen.astype(BF16)
     is_x = core == 0
     scaled = jnp.where(is_x, chosen, chosen * weight).astype(BF16)
 
-    for j in range(1, groups):
-        landed(ra.at[(d + groups - j) % groups], ra_sem.at[j - 1])
     picked = lax.dot_general(
-        scaled, ra[...].reshape(toks, qw), TN, preferred_element_type=F32
+        scaled, ra[:, :, 0:qw].reshape(toks, qw), TN, preferred_element_type=F32
     ).astype(BF16)
     sb[...] = picked.reshape(experts, most, qw)
-    rb[core, y, 0] = picked[0:most]
-
-    def target_of(i, sign):
-        k, dx = i // xs, i % xs
-        dz = (k + 1) // 2 * (2 * (k % 2) - 1) * sign
-        return (x + sign * dx + xs) % xs * zs + (z + dz + zs) % zs
-
+    rb[core, y, own_slot] = picked[own_slot * most : (own_slot + 1) * most]
+
+    pl.semaphore_wait(ring_sem, xs - 1)
+    def exchange(g, sign, src, dst, send, recv):
+        for k in range(g * slots // xs, (g + 1) * slots // xs):
+            to_z = rem(z + sign * order[k] + zs, zs)
+
+            def send_rows(dx, carry, k=k, to_z=to_z):
+                to = rem(x + sign * dx + xs, xs) * zs + to_z
+                remote(
+                    src.at[k * xs + dx], dst.at[k * xs + dx], send.at[g], recv.at[g], expert=to
+                ).start()
+                return carry
+
+            lax.fori_loop(1 if order[k] == 0 else 0, xs, send_rows, 0)
+
+    mine_rb = rb.at[core, y]
     for g in range(parts):
-        def send_rows(i, carry, g=g):
-            remote(
-                sb.at[i], rb.at[core, y, i], sb_sem.at[g], rb_sem.at[g],
-                expert=target_of(i, 1),
-            ).start()
-            return carry
-
-        lax.fori_loop(max(1, g * slots), (g + 1) * slots, send_rows, 0)
-
-    first = [max(1, g * slots) for g in range(parts)]
+        exchange(g, 1, sb, mine_rb, sb_sem, rb_sem)
+
+    def arrived(g, ref, sem):
+        low, high = g * slots, (g + 1) * slots
+        if low <= own_slot < high:
+            if own_slot > low:
+                landed(ref.at[pl.ds(low, own_slot - low)], sem)
+            low = own_slot + 1
+        landed(ref.at[pl.ds(low, high - low)], sem)
 
     def part(g, low=0, high=None):
         low, high = g * slots + low, g * slots + (slots if high is None else high)
@@ -170,8 +206,7 @@
         pending.append(copy)
 
     def stage_own(g):
-        count = (g + 1) * slots - first[g]
-        landed(rb.at[core, y, pl.ds(first[g], count)], rb_sem.at[g])
+        arrived(g, mine_rb, rb_sem.at[g])
         mine = rb.at[core, y, part(g)]
         go(remote(mine, mine, sy_sem.at[g, 0], ry_sem.at[g, 0], dp=up))
         go(remote(mine, mine, sy_sem.at[g, 1], ry_sem.at[g, 1], dp=down))
@@ -234,7 +269,7 @@
         for q in range(QUARTERS):
             sr2[g, q] = (keep[g, q] + rr1[g, q].astype(F32)).astype(BF16)
         for j in range(1, QUARTERS):
-            to = (y + j) % QUARTERS
+            to = rem(y + j, QUARTERS)
             go(remote(
                 sr2.at[g, to], rr2.at[g, j - 1], s2_sem.at[g, j - 1], r2_sem.at[g, j - 1],
                 dp=to * CORES + core,
@@ -248,16 +283,10 @@
             total += rr2[g, j - 1].astype(F32)
         total = total.astype(BF16)
         sr3[part(g)] = total.reshape(slots, most, wide)
-        if g == 0:
-            rr3[0] = total[0:most]
-
-        def send_back(i, carry):
-            remote(
-                sr3.at[i], rr3.at[i], s3_sem.at[g], r3_sem.at[g], expert=target_of(i, -1)
-            ).start()
-            return carry
-
-        lax.fori_loop(first[g], (g + 1) * slots, send_back, 0)
+        if g * slots <= own_slot < (g + 1) * slots:
+            at = (own_slot - g * slots) * most
+            rr3[own_slot] = total[at : at + most]
+        exchange(g, -1, sr3, rr3, s3_sem, r3_sem)
 
     def weight_grads(q):
         grads = lax.dot_general(
@@ -282,8 +311,7 @@
 
     summed = jnp.zeros((toks, wide), F32)
     for g in range(parts):
-        count = (g + 1) * slots - first[g]
-        landed(rr3.at[pl.ds(first[g], count)], r3_sem.at[g])
+        arrived(g, rr3, r3_sem.at[g])
         summed += jnp.dot(
             sel_ref[:, g * rows : (g + 1) * rows],
             rr3[part(g)].reshape(rows, wide),
@@ -292,16 +320,15 @@
     sf[...] = summed.astype(BF16).reshape(groups, per, wide)
     rf[d] = sf[d]
     for j in range(1, groups):
-        p = (d + j) % groups
+        p = rem(d + j, groups)
         go(remote(sf.at[p], rf.at[d], sf_sem.at[j - 1], rf_sem.at[j - 1], dp=p))
-    for copy in sent_i + sent_a + pending[: -(groups - 1)]:
+    for copy in sent_a + pending[: -(groups - 1)]:
         copy.wait_send()
     for g in range(parts):
-        count = (g + 1) * slots - first[g]
-        landed(sb.at[pl.ds(first[g], count)], sb_sem.at[g])
-        landed(sr3.at[pl.ds(first[g], count)], s3_sem.at[g])
+        arrived(g, sb, sb_sem.at[g])
+        arrived(g, sr3, s3_sem.at[g])
     for j in range(1, groups):
-        landed(rf.at[(d + groups - j) % groups], rf_sem.at[j - 1])
+        landed(rf.at[rem(d + groups - j, groups)], rf_sem.at[j - 1])
     for p in range(groups):
         at, size = p // CORES * qw + p % CORES * wide, (wide, narrow)[p % CORES]
         out_t[0, :, at : at + size] = rf[p, :, 0:size]
@@ -328,15 +355,13 @@
             jax.ShapeDtypeStruct(w_gate.shape, BF16),
             jax.ShapeDtypeStruct(w_up.shape, BF16),
         ),
-        in_specs=[vmem] * 4 + [hbm] * 3,
+        in_specs=[hbm] * 7,
         out_specs=(vmem, vmem, vmem),
         scratch_shapes=[
             pltpu.VMEM((width, 2 * hid), BF16),
             pltpu.VMEM((hid, width), BF16),
-            pltpu.VMEM((groups, per, qw), BF16),
-            pltpu.VMEM((groups, per, qw), BF16),
-            pltpu.VMEM((2, per, 128), F32),
-            pltpu.VMEM((groups, 2, per, 128), F32),
+            pltpu.VMEM((groups, per, qw + 256), BF16),
+            pltpu.VMEM((groups, per, qw + 256), BF16),
             pltpu.VMEM((experts, most, qw), BF16),
             pltpu.VMEM((CORES, QUARTERS, experts, most, qw), BF16),
             pltpu.VMEM((experts * most, 2 * hid), BF16),
@@ -350,9 +375,13 @@
             pltpu.VMEM((groups, per, wide), BF16),
             pltpu.VMEM((groups, per, wide), BF16),
             pltpu.VMEM((toks, experts * most), BF16),
+            pltpu.VMEM(tokens.shape, BF16),
+            pltpu.VMEM(grad_out.shape, BF16),
+            pltpu.VMEM(routes.shape, jnp.int32),
+            pltpu.VMEM(gate_scores.shape, BF16),
+            dma((4,)),
             dma((3,)),
-            dma((groups - 1,)),
-            dma((groups - 1,)),
+            pltpu.SemaphoreType.REGULAR,
             dma((groups - 1,)),
             dma((groups - 1,)),
             dma((parts,)),
@@ -371,7 +400,7 @@
             dma((groups - 1,)),
         ],
         compiler_params=pltpu.CompilerParams(
-            collective_id=0, has_side_effects=True, vmem_limit_bytes=48 * 1024 * 1024
+            collective_id=0, has_side_effects=True, vmem_limit_bytes=60 * 1024 * 1024
         ),
         cost_estimate=pl.CostEstimate(
             flops=14 * experts * most * width * hid, bytes_accessed=10 * width * hid,

time: 98 us -> 88.2 us (0.900); the launches traced: 96.7 us -> 87.9 us
  local copies, waits for them, and re-layouts: 9 us -> 4.61 us
  Pallas kernels: 87 us -> 82.7 us
    unnamed x17 -> x5, local copies, waits for them, and re-layouts: 9 us -> 4.61 us
    pallas_call x1, Pallas kernels: 87 us -> 82.7 us  [on_device(): pl.pallas_call(functools.partial(kernel, c), out_shape=(jax.ShapeDtypeStr...]
where the time goes in v2:
time: 88.2 us; the launch traced here: 87.9 us
  Pallas kernels  82.7 us (94%)
  local copies, waits for them, and re-layouts  4.61 us (5%)
    pallas_call x1, Pallas kernels, on_device(): pl.pallas_call(functools.partial(kernel, c), out_shape=(jax.ShapeDtypeStr...  82.7 us
    unnamed x5, local copies, waits for them, and re-layouts  4.61 us

profile of v2, /device:TPU:1, one launch (start us, length us, event | category | flops | bytes accessed | tf_op | source)
XLA Modules:
  0.0 87.9 jit_solution(6431856623248753125)
XLA Ops:
  0.6 82.7 %shard_map.94 = (bf16[1,8,3584]{2,1,0:T(8,128)(2,1)}, bf16[1,3584,128]{2,1,0:T(8,128)(2,1)}, bf16[1,3584,128]{2,1,0:T(8,128)(2,1)}) custom-call(bf16[1,8,3584]{2,1,0:T(8,128)(2,1)} %tok_hbm.1, bf16[1,8,3584]{2,1,0:T(8,128)(2,1)} %dy_hbm.1, s32[1,8,8]{2,1,0:T(8,128)} %routes_hbm.1, bf16[1,8,8]{2,1,0:T(8,128)(2,1)} %scores_hbm.1, ...), custom_call_target="tpu_custom_call" | custom-call | flops 1644167168 | bytes 4587520 | tf_op jit(solution)/shard_map/pallas_call | solution.py:351
  83.3 1.4 %copy.13 = bf16[1,8,3584]{2,1,0:T(8,128)(2,1)} copy(bf16[1,8,3584]{2,1,0:T(8,128)(2,1)} %get-tuple-element.6) | data formatting | bytes 114688
  84.8 0.0 copy-start
  84.8 2.2 %copy.14 = bf16[1,3584,128]{2,1,0:T(8,128)(2,1)} copy(bf16[1,3584,128]{2,1,0:T(8,128)(2,1)} %get-tuple-element.7) | data formatting | bytes 1835008
  87.0 0.0 copy-done
  87.0 0.9 %copy.15 = bf16[1,3584,128]{2,1,0:T(8,128)(2,1)} copy(bf16[1,3584,128]{2,1,0:T(8,128)(2,1)S(1)} %copy-done) | data formatting | bytes 1835008
Async XLA Ops:
  84.8 2.2 %copy-start = (bf16[1,3584,128]{2,1,0:T(8,128)(2,1)S(1)}, bf16[1,3584,128]{2,1,0:T(8,128)(2,1)}, u32[]{:S(2)}) copy-start(bf16[1,3584,128]{2,1,0:T(8,128)(2,1)} %get-tuple-element.8) | copy-start | bytes 2752516

commit v3 on v2

--- a/solution.py
+++ b/solution.py
@@ -10,7 +10,15 @@
 ROUTED = 256
 CORES = 2
 QUARTERS = 4
-PARTS = 8
+SIZES = (2, 2, 2, 2, 2, 2, 2, 2)
+RELAYED = 0
+PLAN = (
+    (0, 0), (0, 1), (0, 2), (1, 0), (0, 3), (2, 0), (1, 1), (3, 0),
+    (2, 1), (0, 4), (1, 2), (3, 1), (2, 2), (1, 3), (0, 5), (3, 2),
+    (2, 3), (4, 0), (3, 3), (1, 4), (0, 6), (2, 4), (4, 1), (3, 4),
+    (1, 5), (0, 7), (2, 5), (4, 2), (4, 3), (3, 5), (1, 6), (2, 6),
+    (4, 4), (3, 6), (1, 7), (2, 7), (4, 5), (4, 6), (3, 7), (4, 7),
+)
 MESH = pl.DeviceIdType.MESH
 F32, BF16 = jnp.float32, jnp.bfloat16
 NT = (((1,), (1,)), ((), ()))
@@ -23,6 +31,11 @@
         steps += [h] if 2 * h == z_size else [h, -h]
     far = sorted(steps, key=lambda s: (-abs(s), -s))
     return far[::-1]
+
+
+def default_plan(parts):
+    stages = (0, 1, 5, 2, 3, 4) if RELAYED else (0, 1, 2, 3, 4)
+    return [(stage, g) for g in range(parts) for stage in stages]
 
 
 def shape_of(mesh_experts, columns_z, width, tok_col, top, hidden):
@@ -32,10 +45,11 @@
     quarter = width // QUARTERS
     tiles = quarter // 128
     wide = (tiles + 1) // 2 * 128
-    parts = min(PARTS, z_size)
+    sizes = SIZES if sum(SIZES) == z_size else (1,) * z_size
+    starts = [sum(sizes[:g]) * x_size for g in range(len(sizes) + 1)]
     return dict(
-        order=order_of(z_size), xs=x_size, zs=z_size, most=most, qw=quarter, wide=wide, parts=parts,
-        slots=mesh_experts // parts, experts=mesh_experts, toks=tok_col, top=top, hid=hidden,
+        order=order_of(z_size), xs=x_size, zs=z_size, most=most, qw=quarter, wide=wide, starts=starts,
+        experts=mesh_experts, toks=tok_col, top=top, hid=hidden,
     )
 
 
@@ -47,13 +61,13 @@
     sy_sem, ry_sem, sc_sem, rc_sem, s1_sem, r1_sem, s2_sem, r2_sem, s3_sem, r3_sem,
     sf_sem, rf_sem,
 ):
-    xs, zs, most, qw, wide, parts = c["xs"], c["zs"], c["most"], c["qw"], c["wide"], c["parts"]
-    slots, experts, toks, hid = c["slots"], c["experts"], c["toks"], c["hid"]
+    xs, zs, most, qw, wide, starts = c["xs"], c["zs"], c["most"], c["qw"], c["wide"], c["starts"]
+    experts, toks, hid = c["experts"], c["toks"], c["hid"]
+    parts = len(starts) - 1
     narrow = qw - wide
     order = c["order"]
     own_slot = order.index(0) * xs
     top = c["top"]
-    rows = slots * most
     groups = CORES * QUARTERS
     per = toks // groups
     d = lax.axis_index("dp")
@@ -170,7 +184,7 @@
 
     pl.semaphore_wait(ring_sem, xs - 1)
     def exchange(g, sign, src, dst, send, recv):
-        for k in range(g * slots // xs, (g + 1) * slots // xs):
+        for k in range(starts[g] // xs, starts[g + 1] // xs):
             to_z = rem(z + sign * order[k] + zs, zs)
 
             def send_rows(dx, carry, k=k, to_z=to_z):
@@ -187,18 +201,23 @@
         exchange(g, 1, sb, mine_rb, sb_sem, rb_sem)
 
     def arrived(g, ref, sem):
-        low, high = g * slots, (g + 1) * slots
+        low, high = starts[g], starts[g + 1]
         if low <= own_slot < high:
             if own_slot > low:
                 landed(ref.at[pl.ds(low, own_slot - low)], sem)
             low = own_slot + 1
         landed(ref.at[pl.ds(low, high - low)], sem)
 
-    def part(g, low=0, high=None):
-        low, high = g * slots + low, g * slots + (slots if high is None else high)
+    def part(g, piece=None):
+        low, high = starts[g], starts[g + 1]
+        middle = (low + high) // 2
+        if piece is not None:
+            low, high = (low, middle) if piece == 0 else (middle, high)
         return pl.ds(low, high - low)
 
-    half = slots // 2
+    def rows_of(g):
+        return pl.ds(starts[g] * most, (starts[g + 1] - starts[g]) * most)
+
     pending = []
 
     def go(copy):
@@ -210,24 +229,33 @@
         mine = rb.at[core, y, part(g)]
         go(remote(mine, mine, sy_sem.at[g, 0], ry_sem.at[g, 0], dp=up))
         go(remote(mine, mine, sy_sem.at[g, 1], ry_sem.at[g, 1], dp=down))
+        if g >= RELAYED:
+            go(remote(mine, mine, sy_sem.at[g, 2], ry_sem.at[g, 2], dp=far_y * CORES + core))
         go(remote(mine, mine, sc_sem.at[g, 0], rc_sem.at[g, 0], dp=other))
 
     def stage_near(g):
         low = rb.at[core, down_y, part(g)]
         landed(low, ry_sem.at[g, 0])
-        piece = rb.at[core, down_y, part(g, 0, half)]
-        go(remote(piece, piece, sy_sem.at[g, 2], ry_sem.at[g, 2], dp=up))
+        if g < RELAYED:
+            piece = rb.at[core, down_y, part(g, 0)]
+            go(remote(piece, piece, sy_sem.at[g, 2], ry_sem.at[g, 2], dp=up))
         go(remote(low, low, sc_sem.at[g, 1], rc_sem.at[g, 1], dp=other))
         high = rb.at[core, up_y, part(g)]
         landed(high, ry_sem.at[g, 1])
-        piece = rb.at[core, up_y, part(g, half)]
-        go(remote(piece, piece, sy_sem.at[g, 3], ry_sem.at[g, 3], dp=down))
+        if g < RELAYED:
+            piece = rb.at[core, up_y, part(g, 1)]
+            go(remote(piece, piece, sy_sem.at[g, 3], ry_sem.at[g, 3], dp=down))
         go(remote(high, high, sc_sem.at[g, 2], rc_sem.at[g, 2], dp=other))
+        if g >= RELAYED:
+            stage_far(g)
 
     def stage_far(g):
-        landed(rb.at[core, far_y, part(g, 0, half)], ry_sem.at[g, 2])
-        landed(rb.at[core, far_y, part(g, half)], ry_sem.at[g, 3])
         whole = rb.at[core, far_y, part(g)]
+        if g < RELAYED:
+            landed(rb.at[core, far_y, part(g, 0)], ry_sem.at[g, 2])
+            landed(rb.at[core, far_y, part(g, 1)], ry_sem.at[g, 3])
+        else:
+            landed(whole, ry_sem.at[g, 2])
         go(remote(whole, whole, sc_sem.at[g, 3], rc_sem.at[g, 3], dp=other))
 
     def stage_compute(g):
@@ -236,6 +264,8 @@
                 load.wait()
         for at, which in enumerate((y, down_y, up_y, far_y)):
             landed(rb.at[1 - core, which, part(g)], rc_sem.at[g, at])
+        mine = rows_of(g)
+        rows = mine.size
         gu = jnp.zeros((rows, 2 * hid), F32)
         dh = jnp.zeros((rows, hid), F32)
         for q in range(QUARTERS):
@@ -251,7 +281,7 @@
         dgate = dh * upv * sig * (1.0 + gate * (1.0 - sig))
         dup = dh * gate * sig
         both = jnp.concatenate([dgate.astype(BF16), dup.astype(BF16)], axis=1)
-        dd[g * rows : (g + 1) * rows, :] = both
+        dd[mine, :] = both
         for q in range(QUARTERS):
             back = lax.dot_general(
                 both, wcat[q * qw : (q + 1) * qw, :], NT, preferred_element_type=F32
@@ -260,31 +290,33 @@
             right = back[:, wide:qw]
             if narrow < wide:
                 right = jnp.concatenate([right, jnp.zeros((rows, wide - narrow), F32)], axis=1)
-            keep[g, q] = jnp.where(is_x, left, right)
-            sr1[g, q] = jnp.where(is_x, right, left).astype(BF16)
-        go(remote(sr1.at[g], rr1.at[g], s1_sem.at[g], r1_sem.at[g], dp=other))
+            keep[q, mine] = jnp.where(is_x, left, right)
+            sr1[q, mine] = jnp.where(is_x, right, left).astype(BF16)
+        go(remote(sr1.at[:, mine], rr1.at[:, mine], s1_sem.at[g], r1_sem.at[g], dp=other))
 
     def stage_chip(g):
-        landed(rr1.at[g], r1_sem.at[g])
+        mine = rows_of(g)
+        landed(rr1.at[:, mine], r1_sem.at[g])
         for q in range(QUARTERS):
-            sr2[g, q] = (keep[g, q] + rr1[g, q].astype(F32)).astype(BF16)
+            sr2[q, mine] = (keep[q, mine] + rr1[q, mine].astype(F32)).astype(BF16)
         for j in range(1, QUARTERS):
             to = rem(y + j, QUARTERS)
             go(remote(
-                sr2.at[g, to], rr2.at[g, j - 1], s2_sem.at[g, j - 1], r2_sem.at[g, j - 1],
+                sr2.at[to, mine], rr2.at[j - 1, mine], s2_sem.at[g, j - 1], r2_sem.at[g, j - 1],
                 dp=to * CORES + core,
             ))
 
     def stage_back(g):
+        mine = rows_of(g)
         for j in range(1, QUARTERS):
-            landed(rr2.at[g, j - 1], r2_sem.at[g, j - 1])
-        total = keep[g, y] + rr1[g, y].astype(F32)
+            landed(rr2.at[j - 1, mine], r2_sem.at[g, j - 1])
+        total = keep[y, mine] + rr1[y, mine].astype(F32)
         for j in range(1, QUARTERS):
-            total += rr2[g, j - 1].astype(F32)
+            total += rr2[j - 1, mine].astype(F32)
         total = total.astype(BF16)
-        sr3[part(g)] = total.reshape(slots, most, wide)
-        if g * slots <= own_slot < (g + 1) * slots:
-            at = (own_slot - g * slots) * most
+        sr3[part(g)] = total.reshape(mine.size // most, most, wide)
+        if starts[g] <= own_slot < starts[g + 1]:
+            at = (own_slot - starts[g]) * most
             rr3[own_slot] = total[at : at + most]
         exchange(g, -1, sr3, rr3, s3_sem, r3_sem)
 
@@ -295,26 +327,30 @@
         out_g[0, q * qw : (q + 1) * qw, :] = grads[:, 0:hid].astype(BF16)
         out_u[0, q * qw : (q + 1) * qw, :] = grads[:, hid : 2 * hid].astype(BF16)
 
-    stages = (stage_own, stage_near, stage_far, stage_compute, stage_chip, stage_back)
-    for step in range(parts + len(stages) - 1):
-        for lag, stage in enumerate(stages):
-            if 0 <= step - lag < parts:
-                stage(step - lag)
-        done = step - (parts - 1) - 3
-        if done == 0:
+    def stages_of(g):
+        tail = [stage_compute, stage_chip, stage_back]
+        return [stage_own, stage_near] + ([stage_far] if g < RELAYED else []) + tail
+
+    for stage, g in PLAN if parts == len(SIZES) else default_plan(parts):
+        (stage_own, stage_near, stage_compute, stage_chip, stage_back, stage_far)[stage](g)
+        if stage == 2 and g == parts - 1:
             weight_grads(0)
-        elif done == 1:
+        if stage == 3 and g == parts - 1:
             weight_grads(1)
-        elif done == 2:
-            weight_grads(2)
-            weight_grads(3)
+    weight_grads(2)
+    weight_grads(3)
+
+    for copy in sent_a + pending:
+        copy.wait_send()
+    for g in range(parts):
+        arrived(g, sb, sb_sem.at[g])
 
     summed = jnp.zeros((toks, wide), F32)
     for g in range(parts):
         arrived(g, rr3, r3_sem.at[g])
         summed += jnp.dot(
-            sel_ref[:, g * rows : (g + 1) * rows],
-            rr3[part(g)].reshape(rows, wide),
+            sel_ref[:, starts[g] * most : starts[g + 1] * most],
+            rr3[part(g)].reshape(rows_of(g).size, wide),
             preferred_element_type=F32,
         )
     sf[...] = summed.astype(BF16).reshape(groups, per, wide)
@@ -322,10 +358,7 @@
     for j in range(1, groups):
         p = rem(d + j, groups)
         go(remote(sf.at[p], rf.at[d], sf_sem.at[j - 1], rf_sem.at[j - 1], dp=p))
-    for copy in sent_a + pending[: -(groups - 1)]:
-        copy.wait_send()
     for g in range(parts):
-        arrived(g, sb, sb_sem.at[g])
         arrived(g, sr3, s3_sem.at[g])
     for j in range(1, groups):
         landed(rf.at[rem(d + groups - j, groups)], rf_sem.at[j - 1])
@@ -343,8 +376,8 @@
     hid = w_gate.shape[2]
     toks = per * groups
     c = shape_of(experts, z_size, width, toks, routes.shape[2], hid)
-    most, qw, wide, parts, slots = c["most"], c["qw"], c["wide"], c["parts"], c["slots"]
-    rows = slots * most
+    most, qw, wide, parts = c["most"], c["qw"], c["wide"], len(c["starts"]) - 1
+    rows = experts * most
     vmem = pl.BlockSpec(memory_space=pltpu.VMEM)
     hbm = pl.BlockSpec(memory_space=pl.ANY)
     dma = pltpu.SemaphoreType.DMA
@@ -365,11 +398,11 @@
             pltpu.VMEM((experts, most, qw), BF16),
             pltpu.VMEM((CORES, QUARTERS, experts, most, qw), BF16),
             pltpu.VMEM((experts * most, 2 * hid), BF16),
-            pltpu.VMEM((parts, QUARTERS, rows, wide), F32),
-            pltpu.VMEM((parts, QUARTERS, rows, wide), BF16),
-            pltpu.VMEM((parts, QUARTERS, rows, wide), BF16),
-            pltpu.VMEM((parts, QUARTERS, rows, wide), BF16),
-            pltpu.VMEM((parts, QUARTERS - 1, rows, wide), BF16),
+            pltpu.VMEM((QUARTERS, rows, wide), F32),
+            pltpu.VMEM((QUARTERS, rows, wide), BF16),
+            pltpu.VMEM((QUARTERS, rows, wide), BF16),
+            pltpu.VMEM((QUARTERS, rows, wide), BF16),
+            pltpu.VMEM((QUARTERS - 1, rows, wide), BF16),
             pltpu.VMEM((experts, most, wide), BF16),
             pltpu.VMEM((experts, most, wide), BF16),
             pltpu.VMEM((groups, per, wide), BF16),

time: 88.2 us -> 85.7 us (0.972)
  Pallas kernels: 82.7 us -> 79.6 us
    pallas_call x1, Pallas kernels: 82.7 us -> 79.6 us  [on_device(): pl.pallas_call(functools.partial(kernel, c), out_shape=(jax.ShapeDtypeStr...]
where the time goes in v3:
time: 85.7 us; the launch traced here: 84.9 us
  Pallas kernels  79.6 us (93%)
  local copies, waits for them, and re-layouts  4.61 us (5%)
    pallas_call x1, Pallas kernels, on_device(): pl.pallas_call(functools.partial(kernel, c), out_shape=(jax.ShapeDtypeStr...  79.6 us
    unnamed x5, local copies, waits for them, and re-layouts  4.61 us

profile of v3, /device:TPU:1, one launch (start us, length us, event | category | flops | bytes accessed | tf_op | source)
XLA Modules:
  0.0 84.9 jit_solution(966406268804204797)
XLA Ops:
  0.6 79.6 %shard_map.94 = (bf16[1,8,3584]{2,1,0:T(8,128)(2,1)}, bf16[1,3584,128]{2,1,0:T(8,128)(2,1)}, bf16[1,3584,128]{2,1,0:T(8,128)(2,1)}) custom-call(bf16[1,8,3584]{2,1,0:T(8,128)(2,1)} %tok_hbm.1, bf16[1,8,3584]{2,1,0:T(8,128)(2,1)} %dy_hbm.1, s32[1,8,8]{2,1,0:T(8,128)} %routes_hbm.1, bf16[1,8,8]{2,1,0:T(8,128)(2,1)} %scores_hbm.1, ...), custom_call_target="tpu_custom_call" | custom-call | flops 1644167168 | bytes 4587520 | tf_op jit(solution)/shard_map/pallas_call | solution.py:384
  80.3 1.4 %copy.13 = bf16[1,8,3584]{2,1,0:T(8,128)(2,1)} copy(bf16[1,8,3584]{2,1,0:T(8,128)(2,1)} %get-tuple-element.6) | data formatting | bytes 114688
  81.7 0.0 copy-start
  81.7 2.2 %copy.14 = bf16[1,3584,128]{2,1,0:T(8,128)(2,1)} copy(bf16[1,3584,128]{2,1,0:T(8,128)(2,1)} %get-tuple-element.7) | data formatting | bytes 1835008
  84.0 0.0 copy-done
  84.0 0.9 %copy.15 = bf16[1,3584,128]{2,1,0:T(8,128)(2,1)} copy(bf16[1,3584,128]{2,1,0:T(8,128)(2,1)S(1)} %copy-done) | data formatting | bytes 1835008
Async XLA Ops:
  81.7 2.2 %copy-start = (bf16[1,3584,128]{2,1,0:T(8,128)(2,1)S(1)}, bf16[1,3584,128]{2,1,0:T(8,128)(2,1)}, u32[]{:S(2)}) copy-start(bf16[1,3584,128]{2,1,0:T(8,128)(2,1)} %get-tuple-element.8) | copy-start | bytes 2752516

commit v4 on v3

--- a/solution.py
+++ b/solution.py
@@ -10,14 +10,13 @@
 ROUTED = 256
 CORES = 2
 QUARTERS = 4
-SIZES = (2, 2, 2, 2, 2, 2, 2, 2)
+SIZES = (3, 3, 3, 3, 2, 2)
 RELAYED = 0
 PLAN = (
-    (0, 0), (0, 1), (0, 2), (1, 0), (0, 3), (2, 0), (1, 1), (3, 0),
-    (2, 1), (0, 4), (1, 2), (3, 1), (2, 2), (1, 3), (0, 5), (3, 2),
-    (2, 3), (4, 0), (3, 3), (1, 4), (0, 6), (2, 4), (4, 1), (3, 4),
-    (1, 5), (0, 7), (2, 5), (4, 2), (4, 3), (3, 5), (1, 6), (2, 6),
-    (4, 4), (3, 6), (1, 7), (2, 7), (4, 5), (4, 6), (3, 7), (4, 7),
+    (0, 0), (0, 1), (1, 0), (0, 2), (2, 0), (1, 1), (3, 0), (2, 1),
+    (0, 3), (1, 2), (3, 1), (2, 2), (4, 0), (0, 4), (3, 2), (1, 3),
+    (2, 3), (4, 1), (0, 5), (3, 3), (1, 4), (2, 4), (4, 2), (3, 4),
+    (1, 5), (2, 5), (4, 3), (3, 5), (4, 4), (4, 5),
 )
 MESH = pl.DeviceIdType.MESH
 F32, BF16 = jnp.float32, jnp.bfloat16
@@ -56,7 +55,7 @@
 def kernel(
     c, tok_hbm, dy_hbm, routes_hbm, scores_hbm, wg_hbm, wu_hbm, wd_hbm,
     out_t, out_g, out_u,
-    wcat, wd, sa, ra, sb, rb, dd, keep, sr1, rr1, sr2, rr2, sr3, rr3, sf, rf, sel_ref,
+    wcat, wd, wt, wdt, sa, ra, sb, rb, dd, keep, sr1, rr1, sr2, rr2, sr3, rr3, sf, rf, sel_ref,
     tok_ref, dy_ref, routes_ref, scores_ref, in_sem, w_sem, ring_sem, sa_sem, ra_sem, sb_sem, rb_sem,
     sy_sem, ry_sem, sc_sem, rc_sem, s1_sem, r1_sem, s2_sem, r2_sem, s3_sem, r3_sem,
     sf_sem, rf_sem,
@@ -218,6 +217,12 @@
     def rows_of(g):
         return pl.ds(starts[g] * most, (starts[g + 1] - starts[g]) * most)
 
+    for load in loads:
+        load.wait()
+    for q in range(QUARTERS):
+        cols = slice(q * qw, (q + 1) * qw)
+        wt[:, cols] = wcat[cols, :].T
+        wdt[cols, :] = wd[:, cols].T
     pending = []
 
     def go(copy):
@@ -259,9 +264,6 @@
         go(remote(whole, whole, sc_sem.at[g, 3], rc_sem.at[g, 3], dp=other))
 
     def stage_compute(g):
-        if g == 0:
-            for load in loads:
-                load.wait()
         for at, which in enumerate((y, down_y, up_y, far_y)):
             landed(rb.at[1 - core, which, part(g)], rc_sem.at[g, at])
         mine = rows_of(g)
@@ -273,8 +275,8 @@
             gu += jnp.dot(
                 rb[0, q, part(g)].reshape(rows, qw), wcat[cols, :], preferred_element_type=F32
             )
-            dh += lax.dot_general(
-                rb[1, q, part(g)].reshape(rows, qw), wd[:, cols], NT, preferred_element_type=F32
+            dh += jnp.dot(
+                rb[1, q, part(g)].reshape(rows, qw), wdt[cols, :], preferred_element_type=F32
             )
         gate, upv = gu[:, 0:hid], gu[:, hid : 2 * hid]
         sig = jax.nn.sigmoid(gate)
@@ -283,8 +285,8 @@
         both = jnp.concatenate([dgate.astype(BF16), dup.astype(BF16)], axis=1)
         dd[mine, :] = both
         for q in range(QUARTERS):
-            back = lax.dot_general(
-                both, wcat[q * qw : (q + 1) * qw, :], NT, preferred_element_type=F32
+            back = jnp.dot(
+                both, wt[:, q * qw : (q + 1) * qw], preferred_element_type=F32
             )
             left = back[:, 0:wide]
             right = back[:, wide:qw]
@@ -393,6 +395,8 @@
         scratch_shapes=[
             pltpu.VMEM((width, 2 * hid), BF16),
             pltpu.VMEM((hid, width), BF16),
+            pltpu.VMEM((2 * hid, width), BF16),
+            pltpu.VMEM((width, hid), BF16),
             pltpu.VMEM((groups, per, qw + 256), BF16),
             pltpu.VMEM((groups, per, qw + 256), BF16),
             pltpu.VMEM((experts, most, qw), BF16),

time: 85.7 us -> 85 us (level)
  no operation moved by 1% of the time
where the time goes in v4:
time: 85 us; the launch traced here: 84.5 us
  Pallas kernels  79.2 us (93%)
  local copies, waits for them, and re-layouts  4.61 us (5%)
    pallas_call x1, Pallas kernels, on_device(): pl.pallas_call(functools.partial(kernel, c), out_shape=(jax.ShapeDtypeStr...  79.2 us
    unnamed x5, local copies, waits for them, and re-layouts  4.61 us

profile of v4, /device:TPU:1, one launch (start us, length us, event | category | flops | bytes accessed | tf_op | source)
XLA Modules:
  0.0 84.5 jit_solution(16156297828944249406)
XLA Ops:
  0.6 79.2 %shard_map.94 = (bf16[1,8,3584]{2,1,0:T(8,128)(2,1)}, bf16[1,3584,128]{2,1,0:T(8,128)(2,1)}, bf16[1,3584,128]{2,1,0:T(8,128)(2,1)}) custom-call(bf16[1,8,3584]{2,1,0:T(8,128)(2,1)} %tok_hbm.1, bf16[1,8,3584]{2,1,0:T(8,128)(2,1)} %dy_hbm.1, s32[1,8,8]{2,1,0:T(8,128)} %routes_hbm.1, bf16[1,8,8]{2,1,0:T(8,128)(2,1)} %scores_hbm.1, ...), custom_call_target="tpu_custom_call" | custom-call | flops 1644167168 | bytes 4587520 | tf_op jit(solution)/shard_map/pallas_call | solution.py:386
  79.9 1.4 %copy.13 = bf16[1,8,3584]{2,1,0:T(8,128)(2,1)} copy(bf16[1,8,3584]{2,1,0:T(8,128)(2,1)} %get-tuple-element.6) | data formatting | bytes 114688
  81.3 0.0 copy-start
  81.3 2.2 %copy.14 = bf16[1,3584,128]{2,1,0:T(8,128)(2,1)} copy(bf16[1,3584,128]{2,1,0:T(8,128)(2,1)} %get-tuple-element.7) | data formatting | bytes 1835008
  83.6 0.0 copy-done
  83.6 0.9 %copy.15 = bf16[1,3584,128]{2,1,0:T(8,128)(2,1)} copy(bf16[1,3584,128]{2,1,0:T(8,128)(2,1)S(1)} %copy-done) | data formatting | bytes 1835008
Async XLA Ops:
  81.3 2.2 %copy-start = (bf16[1,3584,128]{2,1,0:T(8,128)(2,1)S(1)}, bf16[1,3584,128]{2,1,0:T(8,128)(2,1)}, u32[]{:S(2)}) copy-start(bf16[1,3584,128]{2,1,0:T(8,128)(2,1)} %get-tuple-element.8) | copy-start | bytes 2752516

commit v5 on v4

--- a/solution.py
+++ b/solution.py
@@ -105,7 +105,19 @@
     for load in loads:
         load.start()
 
+    if narrow < wide:
+        rr2[:, :, narrow:wide] = jnp.zeros(rr2.shape[:2] + (wide - narrow,), BF16)
+
     barrier = pltpu.get_barrier_semaphore()
+
+    def greet(j, carry):
+        dz = zs // 2 + div(j + 1, 2) * (2 * rem(j, 2) - 1)
+        pl.semaphore_signal(
+            barrier, inc=1, device_id={"expert": x * zs + rem(z + dz, zs)}, device_id_type=MESH
+        )
+        return carry
+
+    lax.fori_loop(0, zs - 1, greet, 0)
     for j in range(1, groups):
         pl.semaphore_signal(
             barrier, inc=1, device_id={"dp": rem(d + j, groups)}, device_id_type=MESH
@@ -116,13 +128,6 @@
             barrier, inc=1, device_id={"expert": rem(x + j, xs) * zs + z}, device_id_type=MESH
         )
 
-    def greet(j, carry):
-        pl.semaphore_signal(
-            barrier, inc=1, device_id={"expert": x * zs + rem(z + j, zs)}, device_id_type=MESH
-        )
-        return carry
-
-    lax.fori_loop(1, zs, greet, 0)
 
     for load in small:
         load.wait()
@@ -182,6 +187,10 @@
     rb[core, y, own_slot] = picked[own_slot * most : (own_slot + 1) * most]
 
     pl.semaphore_wait(ring_sem, xs - 1)
+    def by_width(act):
+        pl.when(is_x)(lambda: act(wide))
+        pl.when(jnp.logical_not(is_x))(lambda: act(narrow))
+
     def exchange(g, sign, src, dst, send, recv):
         for k in range(starts[g] // xs, starts[g + 1] // xs):
             to_z = rem(z + sign * order[k] + zs, zs)
@@ -301,17 +310,26 @@
         landed(rr1.at[:, mine], r1_sem.at[g])
         for q in range(QUARTERS):
             sr2[q, mine] = (keep[q, mine] + rr1[q, mine].astype(F32)).astype(BF16)
-        for j in range(1, QUARTERS):
-            to = rem(y + j, QUARTERS)
-            go(remote(
-                sr2.at[to, mine], rr2.at[j - 1, mine], s2_sem.at[g, j - 1], r2_sem.at[g, j - 1],
-                dp=to * CORES + core,
-            ))
+        def send_chip(cols):
+            for j in range(1, QUARTERS):
+                to = rem(y + j, QUARTERS)
+                remote(
+                    sr2.at[to, mine, 0:cols], rr2.at[j - 1, mine, 0:cols],
+                    s2_sem.at[g, j - 1], r2_sem.at[g, j - 1], dp=to * CORES + core,
+                ).start()
+
+        by_width(send_chip)
+
+    def landed_chip(g, ref, sems):
+        def wait(cols):
+            for j in range(1, QUARTERS):
+                landed(ref.at[j - 1, rows_of(g), 0:cols], sems.at[g, j - 1])
+
+        by_width(wait)
 
     def stage_back(g):
         mine = rows_of(g)
-        for j in range(1, QUARTERS):
-            landed(rr2.at[j - 1, mine], r2_sem.at[g, j - 1])
+        landed_chip(g, rr2, r2_sem)
         total = keep[y, mine] + rr1[y, mine].astype(F32)
         for j in range(1, QUARTERS):
             total += rr2[j - 1, mine].astype(F32)
@@ -346,6 +364,7 @@
         copy.wait_send()
     for g in range(parts):
         arrived(g, sb, sb_sem.at[g])
+        landed_chip(g, sr2, s2_sem)
 
     summed = jnp.zeros((toks, wide), F32)
     for g in range(parts):

time: 85 us -> 84.6 us (level)
  no operation moved by 1% of the time
where the time goes in v5:
time: 84.6 us; the launch traced here: 83.8 us
  Pallas kernels  78.6 us (93%)
  local copies, waits for them, and re-layouts  4.61 us (5%)
    pallas_call x1, Pallas kernels, on_device(): pl.pallas_call(functools.partial(kernel, c), out_shape=(jax.ShapeDtypeStr...  78.6 us
    unnamed x5, local copies, waits for them, and re-layouts  4.61 us

profile of v5, /device:TPU:1, one launch (start us, length us, event | category | flops | bytes accessed | tf_op | source)
XLA Modules:
  0.0 83.8 jit_solution(1096354342299704013)
XLA Ops:
  0.6 78.6 %shard_map.94 = (bf16[1,8,3584]{2,1,0:T(8,128)(2,1)}, bf16[1,3584,128]{2,1,0:T(8,128)(2,1)}, bf16[1,3584,128]{2,1,0:T(8,128)(2,1)}) custom-call(bf16[1,8,3584]{2,1,0:T(8,128)(2,1)} %tok_hbm.1, bf16[1,8,3584]{2,1,0:T(8,128)(2,1)} %dy_hbm.1, s32[1,8,8]{2,1,0:T(8,128)} %routes_hbm.1, bf16[1,8,8]{2,1,0:T(8,128)(2,1)} %scores_hbm.1, ...), custom_call_target="tpu_custom_call" | custom-call | flops 1644167168 | bytes 4587520 | tf_op jit(solution)/shard_map/pallas_call | solution.py:405
  79.2 1.4 %copy.13 = bf16[1,8,3584]{2,1,0:T(8,128)(2,1)} copy(bf16[1,8,3584]{2,1,0:T(8,128)(2,1)} %get-tuple-element.6) | data formatting | bytes 114688
  80.6 0.0 copy-start
  80.6 2.2 %copy.14 = bf16[1,3584,128]{2,1,0:T(8,128)(2,1)} copy(bf16[1,3584,128]{2,1,0:T(8,128)(2,1)} %get-tuple-element.7) | data formatting | bytes 1835008
  82.9 0.0 copy-done
  82.9 0.9 %copy.15 = bf16[1,3584,128]{2,1,0:T(8,128)(2,1)} copy(bf16[1,3584,128]{2,1,0:T(8,128)(2,1)S(1)} %copy-done) | data formatting | bytes 1835008
Async XLA Ops:
  80.6 2.2 %copy-start = (bf16[1,3584,128]{2,1,0:T(8,128)(2,1)S(1)}, bf16[1,3584,128]{2,1,0:T(8,128)(2,1)}, u32[]{:S(2)}) copy-start(bf16[1,3584,128]{2,1,0:T(8,128)(2,1)} %get-tuple-element.8) | copy-start | bytes 2752516
